TPU v7x, 256 devices: a whole 4x4x8 slice. The times are simulated.
256 devices in a mesh: ctx: 32 (over z_lo, y, core), head: 8 (over z_hi, x).
Axes of the slice: x: 4, y: 4, z: 8 (z_hi: 2, z_lo: 4; z = z_hi * 4 + z_lo), core: 2. Of those that a mesh axis runs over, the one named last changes fastest.
Arguments:
- query_rows: bfloat16 [4096, 4096], P('ctx', 'head'), may hold values from -16 to 16
- key_head_rows: bfloat16 [4096, 1024], P('ctx', 'head'), may hold values from -8 to 8
- value_head_rows: bfloat16 [4096, 1024], P('ctx', 'head'), may hold values from -6 to 6
- positions: int32 [4096], P('ctx'), may hold values from 0 to 4095, each once
- residual: bfloat16 [4096, 4096], P('ctx', 'head'), may hold values from -0.75 to 0.75
- norm_gain: bfloat16 [4096], P('head'), may hold values from 0.099609375 to 1.8984375
- expert_ids: int32 [4096, 2], P('ctx'), may hold values from 0 to 7, all different within a row; in each aligned block of 128 rows (0 to 127, 128 to 255, ...) at most 36 rows name the same one
- gate_fixed: int32 [4096], P('ctx'), may hold values from 6554 to 58982
- w_gate: bfloat16 [4096, 114688], P(None, ('ctx', 'head')), may hold values from -0.09375 to 0.09375
- w_up: bfloat16 [4096, 114688], P(None, ('ctx', 'head')), may hold values from -0.09375 to 0.09375
- w_down: bfloat16 [114688, 4096], P(('ctx', 'head')), may hold values from -0.046875 to 0.046875
Outputs:
- mixed: bfloat16 [4096, 4096], P('ctx', 'head')
Inputs may be any that keep to these rules, and one draw needn't show every extreme that they name: `expert_ids`: within each aligned block of 128 rows (the rows of one index of ctx) no expert is named more than 36 times, a bound that some block reaches; the two experts of a row differ. `positions`: each position of the window appears once.
All inputs are finite; a program needn't handle non-finite values.
Results may differ from a plain program's by a relative error of at most 0.023.
Values may be sent and summed in bfloat16 or wider, within the bound.
A program may use at most 128 MiB of HBM per device.

v0:
```python
import jax
import jax.numpy as jnp
from jax import lax
from jax.sharding import PartitionSpec as P

QUERY_HEADS = 32
KEY_VALUE_HEADS = 8
HEAD_SIZE = 128
EXPERTS = 8
TOP = 2
CAP = 36


def body(
    query_rows,
    key_head_rows,
    value_head_rows,
    positions,
    residual,
    norm_gain,
    expert_ids,
    gate_fixed,
    w_gate,
    w_up,
    w_down,
):
    tok_rows = query_rows.shape[0]
    kv_local = key_head_rows.shape[1] // HEAD_SIZE
    query_group_size = QUERY_HEADS // KEY_VALUE_HEADS
    feature_count = query_rows.shape[1]
    q_heads = (
        query_rows.reshape(tok_rows, kv_local, query_group_size, HEAD_SIZE)
        .transpose(1, 2, 0, 3)
        .reshape(kv_local, query_group_size * tok_rows, HEAD_SIZE)
    )
    q_places = jnp.tile(positions, query_group_size)
    row_max = jnp.full((kv_local, query_group_size * tok_rows), -1e30, jnp.float32)
    k_piece = lax.all_gather(key_head_rows, "ctx", axis=0, tiled=True)
    v_piece = lax.all_gather(value_head_rows, "ctx", axis=0, tiled=True)
    p_piece = lax.all_gather(positions, "ctx", axis=0, tiled=True)
    piece_rows = k_piece.shape[0]
    k_heads = k_piece.reshape(piece_rows, kv_local, HEAD_SIZE).transpose(1, 0, 2)
    v_heads = v_piece.reshape(piece_rows, kv_local, HEAD_SIZE).transpose(1, 0, 2)
    scores = jnp.einsum(
        "hqd,hkd->hqk", q_heads, k_heads, preferred_element_type=jnp.float32
    ) * HEAD_SIZE ** (-0.5)
    visible = p_piece[None, :] <= q_places[:, None]
    scores = jnp.where(visible[None], scores, -jnp.inf)
    new_max = jnp.maximum(row_max, jnp.max(scores, axis=2))
    exp_scores = jnp.exp(scores - new_max[:, :, None])
    row_sum = jnp.sum(exp_scores, axis=2)
    weighted = jnp.einsum(
        "hqk,hkd->hqd", exp_scores.astype(jnp.bfloat16), v_heads, preferred_element_type=jnp.float32
    )
    row_max, row_sum, weighted = (new_max, row_sum, weighted)
    attention = (
        (weighted / row_sum[:, :, None])
        .reshape(kv_local, query_group_size, tok_rows, HEAD_SIZE)
        .transpose(2, 0, 1, 3)
        .reshape(tok_rows, feature_count)
        .astype(jnp.bfloat16)
    )
    stream = residual.astype(jnp.float32) + attention.astype(jnp.float32)
    expert_range = jnp.arange(EXPERTS, dtype=jnp.int32)
    first_weight = gate_fixed.astype(jnp.float32) / 65536.0
    pair_weights = jnp.stack([first_weight, 1.0 - first_weight], axis=1)
    expert_hits = (expert_ids[:, :, None] == expert_range).astype(jnp.int32)
    flat_hits = expert_hits.reshape(tok_rows * TOP, EXPERTS)
    slot_ranks = jnp.cumsum(flat_hits, axis=0) - flat_hits
    slot_index = jnp.sum(slot_ranks * flat_hits, axis=1).reshape(tok_rows, TOP)
    slot_target = expert_ids * CAP + slot_index
    placed = slot_target[:, :, None] == jnp.arange(EXPERTS * CAP, dtype=jnp.int32)
    pick_table = jnp.any(placed, axis=1).astype(jnp.bfloat16)
    combine_weights = jnp.sum(jnp.where(placed, pair_weights[:, :, None], 0.0), axis=1)
    ctx_count = lax.axis_size("ctx")
    sub_count = ctx_count // EXPERTS
    attn_all, resid_all, gain_all = (
        lax.all_gather(attention, "head", axis=1, tiled=True),
        lax.all_gather(residual, "head", axis=1, tiled=True),
        lax.all_gather(norm_gain.reshape(1, -1), "head", axis=1, tiled=True),
    )
    stream_all = resid_all.astype(jnp.float32) + attn_all.astype(jnp.float32)
    mean_sq = jnp.mean(stream_all * stream_all, axis=1, keepdims=True)
    normed = (stream_all * lax.rsqrt(mean_sq + 1e-05) * gain_all.astype(jnp.float32)).astype(
        jnp.bfloat16
    )
    piece_width = normed.shape[1]
    gathered_rows = jnp.einsum(
        "tr,tf->rf", pick_table, normed, preferred_element_type=jnp.float32
    ).astype(jnp.bfloat16)
    copies = jnp.broadcast_to(
        gathered_rows.reshape(EXPERTS, 1, CAP, piece_width), (EXPERTS, sub_count, CAP, piece_width)
    )
    arrived = lax.all_to_all(
        copies.reshape(ctx_count, CAP, piece_width), "ctx", split_axis=0, concat_axis=0, tiled=True
    )
    expert_rows = arrived.reshape(-1, arrived.shape[2])
    gate_part = jnp.dot(expert_rows, w_gate, preferred_element_type=jnp.float32)
    up_part = jnp.dot(expert_rows, w_up, preferred_element_type=jnp.float32)
    hidden = (jax.nn.silu(gate_part) * up_part).astype(jnp.bfloat16)
    down_terms = jnp.dot(hidden, w_down, preferred_element_type=jnp.float32)
    shares = lax.psum_scatter(
        down_terms.astype(jnp.bfloat16), "head", scatter_dimension=1, tiled=True
    ).astype(jnp.float32)
    returned = lax.all_to_all(
        shares.reshape(ctx_count, CAP, -1).astype(jnp.bfloat16),
        "ctx",
        split_axis=0,
        concat_axis=0,
        tiled=True,
    ).astype(jnp.float32)
    summed = jnp.sum(returned.reshape(EXPERTS, sub_count, CAP, -1), axis=1).reshape(
        EXPERTS * CAP, -1
    )
    expert_mix = jnp.dot(
        combine_weights, summed, precision=lax.Precision.HIGHEST, preferred_element_type=jnp.float32
    )
    return (stream + expert_mix).astype(jnp.bfloat16)


def solution(mesh):
    in_specs = (
        P("ctx", "head"),
        P("ctx", "head"),
        P("ctx", "head"),
        P("ctx"),
        P("ctx", "head"),
        P("head"),
        P("ctx", None),
        P("ctx"),
        P(None, ("ctx", "head")),
        P(None, ("ctx", "head")),
        P(("ctx", "head"), None),
    )
    out_specs = P("ctx", "head")
    return jax.shard_map(body, mesh=mesh, in_specs=in_specs, out_specs=out_specs, check_vma=False)
```

profile of v0, /device:TPU:33, one launch (start us, length us, event | category | flops | bytes accessed | tf_op | source)
XLA Modules:
  0.0 788.5 jit_solution(13222571783382831275)
XLA Ops:
  6.5 0.7 all-gather.8.cloned.1.call-update
  7.3 0.0 all-gather.10.cloned.1.call-start
  7.3 0.7 all-gather.10.cloned.1.call-update
  8.0 0.0 all-gather.12.cloned.1.call-start
  8.1 0.7 all-gather.12.cloned.1.call-update
  8.7 0.0 all-gather.14.cloned.1.call-start
  8.8 0.7 broadcast_bitcast_fusion
  9.4 1.0 copy.45
  10.5 0.1 copy.46
  10.6 37.4 %all-gather.1 = s32[32,1,128]{2,1,0:T(1,128)S(1)} all-gather(s32[1,1,128]{2,1,0:T(1,128)} %bitcast.56), channel_id=1, replica_groups=mesh['ctx'=32,'head'=8] {'ctx'}, dimensions={0}, use_global_device_ids=true | all-gather | bytes 16896 | tf_op jit(solution)/shard_map/all_gather | solution.py:40
  48.0 22.8 %all-gather.8.cloned.1.call-done = bf16[4096,128]{1,0:T(8,128)(2,1)} async-done(((bf16[128,128]{1,0:T(8,128)(2,1)}), bf16[4096,128]{1,0:T(8,128)(2,1)}) %all-gather.8.cloned.1.call-update) | async-done | bytes 1048592 | tf_op jit(solution)/shard_map/all_gather | solution.py:38
  70.8 2.8 fusion.22
  73.6 3.2 copy-done
  76.9 1.3 fusion
  78.1 0.0 copy-start.3
  78.1 52.3 %all-gather.10.cloned.1.call-done = bf16[4096,128]{1,0:T(8,128)(2,1)} async-done(((bf16[128,128]{1,0:T(8,128)(2,1)}), bf16[4096,128]{1,0:T(8,128)(2,1)}) %all-gather.10.cloned.1.call-update) | async-done | bytes 1048592 | tf_op jit(solution)/shard_map/all_gather | solution.py:39
  130.5 4.9 fusion.10
  135.4 0.1 copy.47
  135.5 0.7 copy.55
  136.2 0.0 all-gather.14.cloned.1.call-update
  136.2 0.0 reduce-scatter.2.cloned.1.call-start
  136.3 0.1 copy.48
  136.4 0.1 eq.43
  136.5 0.1 eq.39
  136.7 0.6 reduce-window.6
  137.3 0.2 slice_reduce_fusion
  137.5 0.1 fusion.18
  137.6 0.1 reshape.100
  137.8 0.1 copy.50
  137.8 35.2 %all-gather.2 = bf16[8,1,512]{2,1,0:T(2,128)(2,1)S(1)} all-gather(bf16[1,1,512]{2,1,0:T(2,128)(2,1)S(1)} %reshape.115), channel_id=2, replica_groups=mesh['ctx'=32,'head'=8] {'head'}, dimensions={0}, use_global_device_ids=true | all-gather | bytes 9216 | tf_op jit(solution)/shard_map/all_gather | solution.py:80
  173.1 18.4 %all-gather.12.cloned.1.call-done = bf16[128,4096]{1,0:T(8,128)(2,1)} async-done(((bf16[128,512]{1,0:T(8,128)(2,1)}), bf16[128,4096]{1,0:T(8,128)(2,1)}) %all-gather.12.cloned.1.call-update) | async-done | bytes 1048592 | tf_op jit(solution)/shard_map/all_gather | solution.py:79
  191.5 59.7 %all-gather.14.cloned.1.call-done = bf16[128,4096]{1,0:T(8,128)(2,1)} async-done(((bf16[128,512]{1,0:T(8,128)(2,1)}), bf16[128,4096]{1,0:T(8,128)(2,1)}) %all-gather.14.cloned.1.call-update) | async-done | bytes 1048592 | tf_op jit(solution)/shard_map/all_gather | solution.py:78
  251.2 2.0 multiply_reduce_fusion
  253.2 2.4 convolution_convert_fusion.1
  255.6 2.2 broadcast_in_dim.40
  257.9 7.1 broadcast_in_dim.41
  264.9 236.5 %all_to_all.10 = bf16[32,36,4096]{2,1,0:T(8,128)(2,1)} all-to-all(bf16[32,36,4096]{2,1,0:T(8,128)(2,1)} %bitcast.47), channel_id=1, replica_groups=mesh['ctx'=32,'head'=8] {'ctx'}, dimensions={0} | all-to-all | bytes 18874368 | tf_op jit(solution)/shard_map/all_to_all | solution.py:94
  501.4 13.3 %reshape.103 = bf16[1152,4096]{1,0:T(8,128)(2,1)} reshape(bf16[32,36,4096]{2,1,0:T(8,128)(2,1)} %all_to_all.10) | data formatting | bytes 18874368 | tf_op jit(solution)/shard_map/reshape | solution.py:97
  514.7 9.7 %fusion.23 = f32[1152,448]{0,1:T(8,128)S(1)} fusion(bf16[1152,4096]{1,0:T(8,128)(2,1)} %reshape.103, bf16[4096,448]{0,1:T(8,128)(2,1)} %param.19), kind=kOutput, calls=%fused_computation.42 | convolution fusion | flops 4227858432 | bytes 15171584 | tf_op jit(solution)/shard_map/dot_general | solution.py:98
  524.4 17.4 %convolution_convert_fusion = bf16[1152,4096]{1,0:T(8,128)(2,1)} fusion(bf16[448,4096]{1,0:T(8,128)(2,1)} %param.21, bf16[1152,4096]{1,0:T(8,128)(2,1)} %reshape.103, bf16[4096,448]{0,1:T(8,128)(2,1)} %param.20, f32[1152,448]{0,1:T(8,128)S(1)} %fusion.23), kind=kOutput, calls=%fused_computation | convolution fusion | flops 8463532032 | bytes 28278784 | tf_op jit(solution)/shard_map/dot_general | solution.py:101
  541.7 0.0 reduce-scatter.2.cloned.1.call-update
  541.8 196.7 %reduce-scatter.2.cloned.1.call-done = bf16[1152,512]{1,0:T(8,128)(2,1)} async-done(((bf16[1152,4096]{1,0:T(8,128)(2,1)}), bf16[1152,512]{1,0:T(8,128)(2,1)}) %reduce-scatter.2.cloned.1.call-update) | async-done | bytes 1179664 | tf_op jit(solution)/shard_map/reduce_scatter | solution.py:102
  738.5 2.9 convert_element_type.78
  741.4 6.6 all-to-all-start.1
  748.1 32.2 %all-to-all-done.1 = bf16[32,36,512]{2,1,0:T(8,128)(2,1)S(1)} async-done(((bf16[32,36,512]{2,1,0:T(8,128)(2,1)}), bf16[32,36,512]{2,1,0:T(8,128)(2,1)S(1)}, u32[]{:S(2)}, u32[]{:S(2)}) %all-to-all-start.1) | async-done | bytes 1179680 | tf_op jit(solution)/shard_map/all_to_all | solution.py:105
  780.3 0.2 convert_reduce_fusion
  780.5 0.1 reshape.106
  780.6 1.3 fusion.6
  (21 shorter events, 0.2 us)
Async XLA Ops:
  6.5 64.3 %all-gather.8.cloned.1.call-start = ((), (), s32[]{:S(2)}) async-start(), calls=%async_computation.3 | async-start | bytes 1081344 | tf_op jit(solution)/shard_map/all_gather | solution.py:38
  7.3 123.2 %all-gather.10.cloned.1.call-start = ((), (), s32[]{:S(2)}) async-start(), calls=%async_computation.4 | async-start | bytes 1081344 | tf_op jit(solution)/shard_map/all_gather | solution.py:39
  8.0 183.5 %all-gather.12.cloned.1.call-start = ((), (), s32[]{:S(2)}) async-start(), calls=%async_computation.5 | async-start | bytes 1179648 | tf_op jit(solution)/shard_map/all_gather | solution.py:79
  8.7 242.5 %all-gather.14.cloned.1.call-start = ((), (), s32[]{:S(2)}) async-start(), calls=%async_computation.6 | async-start | bytes 1179648 | tf_op jit(solution)/shard_map/all_gather | solution.py:78
  73.6 3.2 copy-start
  78.1 58.1 %copy-start.2 = (s32[128,2]{0,1:T(2,128)S(1)}, s32[128,2]{0,1:T(2,128)}, u32[]{:S(2)}) copy-start(s32[128,2]{0,1:T(2,128)} %param.17) | copy-start | bytes 3076
  78.1 59.7 %copy-start.3 = (bf16[512]{0:T(512)(128)(2,1)S(1)}, bf16[512]{0:T(512)(128)(2,1)}, u32[]{:S(2)}) copy-start(bf16[512]{0:T(512)(128)(2,1)} %param.16) | copy-start | bytes 3076
  136.2 602.2 %reduce-scatter.2.cloned.1.call-start = ((), (), s32[]{:S(2)}) async-start(), calls=%async_computation.7 | async-start | bytes 10616832 | tf_op jit(solution)/shard_map/reduce_scatter | solution.py:102
  541.8 206.3 %copy-start.4 = (s32[128]{0:T(128)S(1)}, s32[128]{0:T(128)}, u32[]{:S(2)}) copy-start(s32[128]{0:T(128)} %param.18) | copy-start | bytes 1540
  541.8 238.8 %copy-start.1 = (bf16[128,512]{1,0:T(8,128)(2,1)S(1)}, bf16[128,512]{1,0:T(8,128)(2,1)}, u32[]{:S(2)}) copy-start(bf16[128,512]{1,0:T(8,128)(2,1)} %param.15) | copy-start | bytes 393220
  741.4 38.9 %all-to-all-start.1 = ((bf16[32,36,512]{2,1,0:T(8,128)(2,1)}), bf16[32,36,512]{2,1,0:T(8,128)(2,1)S(1)}, u32[]{:S(2)}, u32[]{:S(2)}) async-start(bf16[32,36,512]{2,1,0:T(8,128)(2,1)} %convert_element_type.78), calls=%async_computation.2 | async-start | bytes 2621440 | tf_op jit(solution)/shard_map/all_to_all | solution.py:105
Sparse Core Ops, SparseCore 0:
  9.2 61.5 all-gather.7
  72.7 57.7 all-gather.9
  133.0 58.4 all-gather.11
  193.8 57.3 all-gather.13
  541.9 196.5 reduce-scatter.1
where the time goes:
time: 790 us; the launch traced here: 788 us
  waiting for transfers between devices  384 us (49%)
  blocking collectives  309 us (39%)
  matrix products  38.4 us (5%)
  local copies, waits for them, and re-layouts  32.2 us (4%)
  between operations  13.3 us (2%)
    all_to_all x1, blocking collectives, body(): lax.all_to_all(copies.reshape(ctx_count, CAP, piece_width), 'ctx', split_...  237 us
    reduce_scatter x1, waiting for transfers between devices, body(): lax.psum_scatter(down_terms.astype(jnp.bfloat16), 'head', scatter_dimensi...  197 us
    all_gather x1, waiting for transfers between devices, body(): lax.all_gather(attention, 'head', axis=1, tiled=True)  59.7 us
    all_gather x1, waiting for transfers between devices, body(): v_piece = lax.all_gather(value_head_rows, 'ctx', axis=0, tiled=True)  52.3 us
    all_gather x1, blocking collectives, body(): p_piece = lax.all_gather(positions, 'ctx', axis=0, tiled=True)  37.4 us
    all_gather x1, blocking collectives, body(): lax.all_gather(norm_gain.reshape(1, -1), 'head', axis=1, tiled=True)  35.2 us
    all_to_all x1, waiting for transfers between devices, body(): lax.all_to_all(shares.reshape(ctx_count, CAP, -1).astype(jnp.bfloat16), '...  32.2 us
    all_gather x1, waiting for transfers between devices, body(): k_piece = lax.all_gather(key_head_rows, 'ctx', axis=0, tiled=True)  22.8 us
  transfers between devices with their start and end apart: 6, of which 6 were waited for; matrix products, arithmetic and copies ran while one was open for 2% of the time, Pallas kernels for 0%

commit v1 on v0

v1 whole, which is shorter than its diff:
```python
import jax
import jax.numpy as jnp
from jax import lax
from jax.experimental import pallas as pl
from jax.experimental.pallas import tpu as pltpu
from jax.sharding import PartitionSpec as P

MESH = pl.DeviceIdType.MESH
HEAD_SIZE = 128
CAP = 36
SLOT = 48
EXPERTS = 8
ROWS = 8 * CAP
HALF = 512
QUARTER = ROWS // 2
SCALE = HEAD_SIZE ** (-0.5)
F32 = jnp.float32
BF16 = jnp.bfloat16


class Sems:
    def __init__(self, send, recv):
        self.send, self.recv, self.used = send, recv, 0

    def take(self, count=1):
        at = self.used
        self.used += count
        return at


def dot(a, b):
    return jnp.dot(a, b, preferred_element_type=F32)


def kernel(
    q_ref, k_ref, v_ref, ints_ref, posrow_ref, resid_ref, gain_ref, wg_hbm, wu_hbm, wd_hbm,
    out_ref,
    kv, ssq, stream, pick, cw, gbuf, d1, xb, wg, wu, wd, accg, accu, hid, yb, rq, rh, rf, z, r2s, r2,
    send, recv, local,
):
    c, h = lax.axis_index("ctx"), lax.axis_index("head")
    core, y, zl = lax.rem(c, 2), lax.rem(lax.div(c, 2), 4), lax.div(c, 8)
    yl, yh = lax.rem(y, 2), lax.div(y, 2)
    zh, x = lax.div(h, 4), lax.rem(h, 4)

    def at(zl_=zl, yh_=yh, yl_=yl, core_=core, zh_=zh, x_=x):
        return (zl_ * 8 + (yh_ * 2 + yl_) * 2 + core_, zh_ * 4 + x_)

    right, left = at(x_=lax.rem(x + 1, 4)), at(x_=lax.rem(x + 3, 4))
    across, mate = at(yl_=1 - yl), at(core_=1 - core)
    sems = Sems(send, recv)

    def copy(src, dst, n, device):
        return pltpu.make_async_remote_copy(
            src_ref=src, dst_ref=dst, send_sem=send.at[n], recv_sem=recv.at[n],
            device_id=device, device_id_type=MESH,
        )

    def arrive(dst, n):
        copy(dst, dst, n, mate).wait_recv()

    started = []

    def push(src, dst, n, device):
        copy(src, dst, n, device).start()
        started.append((src, n))

    loads = [
        pltpu.make_async_copy(wg_hbm, wg, local.at[0]),
        pltpu.make_async_copy(wu_hbm, wu, local.at[1]),
        pltpu.make_async_copy(
            wd_hbm.at[:, pl.ds(pl.multiple_of(core * 2048, 128), 2048)], wd.at[0], local.at[2]
        ),
    ]
    for load in loads:
        load.start()

    kv[0, 0, 0:128, :] = k_ref[...]
    kv[0, 0, 128:256, :] = v_ref[...]
    pos = posrow_ref[...]
    pos_hi = lax.shift_right_logical(pos, 6).astype(F32)
    pos_lo = (pos & 63).astype(F32)
    row16 = lax.broadcasted_iota(jnp.int32, (16, 128), 0)
    kv[0, 0, 256:272, :] = jnp.where(row16 == 0, pos_hi, pos_lo).astype(BF16)

    barrier = pltpu.get_barrier_semaphore()
    me16 = zl * 4 + y
    me32 = ((zh * 4 + zl) * 2 + yh) * 2 + core

    def greet(device):
        pl.semaphore_signal(barrier, inc=1, device_id=device, device_id_type=MESH)

    def kv_peer(r):
        j = lax.rem(me16 + r, 16)
        return (lax.div(j, 4) * 8 + lax.rem(j, 4) * 2 + core, h)

    @pl.loop(1, 16)
    def _(r):
        greet(kv_peer(r))

    @pl.loop(1, 8)
    def _(r):
        greet((c, lax.rem(h + r, 8)))

    @pl.loop(1, 32)
    def _(r):
        j = lax.rem(me32 + r, 32)
        greet(
            at(
                zl_=lax.rem(lax.div(j, 4), 4),
                yh_=lax.rem(lax.div(j, 2), 2),
                core_=lax.rem(j, 2),
                zh_=lax.div(j, 16),
            )
        )

    pl.semaphore_wait(barrier, 15 + 7 + 31)

    kv_n, mate_n, wd_n = sems.take(16), sems.take(16), sems.take()

    @pl.loop(1, 16)
    def _(r):
        copy(kv.at[0, 0], kv.at[0, r], kv_n + r, kv_peer(r)).start()

    copy(kv.at[0, 0], kv.at[1, 0], mate_n, mate).start()
    other = pl.multiple_of((1 - core) * 2048, 128)
    wd_move = copy(wd_hbm.at[:, pl.ds(other, 2048)], wd.at[1], wd_n, mate)
    wd_move.start()

    ids0, ids1 = ints_ref[:, 0:1], ints_ref[:, 1:2]
    lane = lax.broadcasted_iota(jnp.int32, (128, 128), 1)
    below = lax.broadcasted_iota(jnp.int32, (128, 128), 0) > lane
    hit0, hit1 = lane == ids0, lane == ids1
    hits = jnp.where(hit0 | hit1, 1.0, 0.0).astype(BF16)
    ranks = dot(jnp.where(below, 1.0, 0.0).astype(BF16), hits)
    slot0 = ids0.astype(F32) * SLOT + jnp.sum(jnp.where(hit0, ranks, 0.0), axis=1, keepdims=True)
    slot1 = ids1.astype(F32) * SLOT + jnp.sum(jnp.where(hit1, ranks, 0.0), axis=1, keepdims=True)
    places = lax.broadcasted_iota(jnp.int32, (128, EXPERTS * SLOT), 1).astype(F32)
    at0, at1 = places == slot0, places == slot1
    pick[...] = jnp.where(at0 | at1, 1.0, 0.0).astype(BF16)
    first = ints_ref[:, 2:3].astype(F32) / 65536.0
    weights = jnp.where(at0, first, 0.0) + jnp.where(at1, 1.0 - first, 0.0)
    coarse = weights.astype(BF16)
    cw[0] = coarse
    cw[1] = (weights - coarse.astype(F32)).astype(BF16)

    q = jnp.concatenate([q_ref[:, 128 * i : 128 * i + 128] for i in range(4)], axis=0)
    q_pos = jnp.concatenate([ints_ref[:, 3:4].astype(F32)] * 4, axis=0)

    def attend(side, group, carry):
        top, total, acc = carry
        part = kv[side, pl.ds(group * 4, 4)]
        keys = part[:, 0:128, :].reshape(512, 128)
        values = part[:, 128:256, :].reshape(512, 128)
        places = part[:, 256:272, :].astype(F32)
        k_pos = jnp.concatenate(
            [places[i, 0:1, :] * 64.0 + places[i, 1:2, :] for i in range(4)], axis=1
        )
        scores = lax.dot_general(q, keys, (((1,), (1,)), ((), ())), preferred_element_type=F32)
        scores = jnp.where(k_pos <= q_pos, scores * SCALE, -1e30)
        new_top = jnp.maximum(top, jnp.max(scores, axis=1, keepdims=True))
        keep = jnp.exp(top - new_top)
        probs = jnp.exp(scores - new_top)
        total = total * keep + jnp.sum(probs, axis=1, keepdims=True)
        acc = acc * keep + dot(probs.astype(BF16), values)
        return new_top, total, acc

    def own_side(group, carry):
        for i in range(4):
            r = group * 4 + i

            @pl.when(r > 0)
            def _(r=r):
                arrive(kv.at[0, r], kv_n + r)
                copy(kv.at[0, r], kv.at[1, r], mate_n + r, mate).start()

        return attend(0, group, carry)

    def mate_side(group, carry):
        for i in range(4):
            r = group * 4 + i
            arrive(kv.at[1, r], mate_n + r)
        return attend(1, group, carry)

    carry = (jnp.full((512, 1), -1e30, F32), jnp.zeros((512, 1), F32), jnp.zeros((512, 128), F32))
    carry = lax.fori_loop(0, 4, own_side, carry)
    _, total, acc = lax.fori_loop(0, 4, mate_side, carry)
    att = (acc / total).astype(BF16).astype(F32)
    att = jnp.concatenate([att[128 * i : 128 * i + 128] for i in range(4)], axis=1)
    flow = resid_ref[...].astype(F32) + att
    stream[...] = flow

    own_sq = jnp.sum(flow * flow, axis=1, keepdims=True)
    ssq[0] = jnp.transpose(jnp.broadcast_to(own_sq, (128, 128)))[0:8, :]
    ssq_n = sems.take(8)

    @pl.loop(1, 8)
    def _(r):
        copy(ssq.at[0], ssq.at[r], ssq_n + r, (c, lax.rem(h + r, 8))).start()

    @pl.loop(1, 8)
    def _(r):
        arrive(ssq.at[r], ssq_n + r)

    all_sq = jnp.sum(ssq[...], axis=0)
    all_sq = jnp.transpose(jnp.concatenate([all_sq] * 16, axis=0))[:, 0:1]
    normed = flow * lax.rsqrt(all_sq / 4096.0 + 1e-05) * gain_ref[...].astype(F32)
    rows = lax.dot_general(
        pick[...], normed.astype(BF16), (((0,), (0,)), ((), ())), preferred_element_type=F32
    ).astype(BF16)
    gbuf[...] = rows.reshape(EXPERTS, SLOT, HALF)

    d1_n = sems.take(16)
    me8 = zl * 2 + yh
    mine = zh * 8 + me8

    @pl.loop(1, 16)
    def _(r):
        j = lax.rem(mine + r, 16)
        e = lax.rem(j, 8)
        device = at(zl_=lax.div(e, 2), yh_=lax.rem(e, 2), zh_=lax.div(j, 8))
        copy(gbuf.at[e], d1.at[zh, me8], d1_n + r, device).start()

    d1[zh, me8] = gbuf[me8]

    @pl.loop(1, 16)
    def _(r):
        j = lax.rem(mine + 16 - r, 16)
        arrive(d1.at[lax.div(j, 8), lax.rem(j, 8)], d1_n + r)

    tight = lax.broadcasted_iota(jnp.int32, (ROWS, 8 * SLOT), 0)
    wide = lax.broadcasted_iota(jnp.int32, (ROWS, 8 * SLOT), 1)
    block = sum([jnp.where(tight >= CAP * i, 1, 0) for i in range(1, 8)])
    compact = jnp.where(wide == tight + block * (SLOT - CAP), 1.0, 0.0).astype(BF16)
    for i in range(2):
        xb[0, 0, 0, i] = dot(compact, d1[i].reshape(8 * SLOT, HALF)).astype(BF16)

    got = {}

    def relay(src, way, rows_of=None):
        side, dy, dx, i = src
        device, to = {
            "r": (right, (0, dy, (dx + 3) % 4, i)),
            "l": (left, (0, dy, (dx + 1) % 4, i)),
            "y": (across, (0, 1 - dy, dx, i)),
            "m": (mate, (1, dy, dx, i)),
        }[way]
        n = sems.take()
        part, there = xb.at[src], xb.at[to]
        if rows_of is not None:
            part = part.at[pl.ds(rows_of * QUARTER, QUARTER)]
            there = there.at[pl.ds(rows_of * QUARTER, QUARTER)]
        push(part, there, n, device)
        got[(*to, rows_of)] = (there, n)

    def landed(slot, rows_of=None):
        there, n = got[(*slot, rows_of)]
        arrive(there, n)

    for load in loads[:2]:
        load.wait()
    accg[...] = jnp.zeros_like(accg)
    accu[...] = jnp.zeros_like(accu)

    def multiply(side, dy, dx):
        xs = lax.rem(x + dx, 4)
        low = pl.ds(pl.multiple_of(xs * HALF, HALF), HALF)
        high = pl.ds(pl.multiple_of(2048 + xs * HALF, HALF), HALF)
        a, b = xb[side, dy, dx, 0], xb[side, dy, dx, 1]
        accg[side, dy] += dot(a, wg[low, :]) + dot(b, wg[high, :])
        accu[side, dy] += dot(a, wu[low, :]) + dot(b, wu[high, :])

    own = [(0, 0, 0, 0), (0, 0, 0, 1)]
    relay(own[0], "r"), relay(own[1], "l"), relay(own[0], "y")
    relay(own[1], "r"), relay(own[0], "l"), relay(own[1], "y")
    relay(own[0], "m"), relay(own[1], "m")
    multiply(0, 0, 0)
    landed((0, 0, 3, 0)), relay((0, 0, 3, 0), "r")
    landed((0, 0, 1, 1)), relay((0, 0, 1, 1), "l"), relay((0, 0, 1, 1), "y")
    landed((0, 1, 0, 0)), relay((0, 1, 0, 0), "r"), relay((0, 1, 0, 0), "l")
    landed((0, 0, 3, 1)), relay((0, 0, 3, 1), "y")
    landed((0, 0, 1, 0)), landed((0, 1, 0, 1))
    for slot in ((0, 3), (0, 1), (1, 0)):
        for i in range(2):
            relay((0, *slot, i), "m")
    landed((1, 0, 0, 0)), landed((1, 0, 0, 1))
    multiply(1, 0, 0)
    multiply(0, 0, 3)
    landed((0, 0, 2, 1)), relay((0, 0, 2, 1), "y"), relay((0, 0, 2, 1), "m")
    landed((0, 1, 3, 0)), relay((0, 1, 3, 0), "r", 0), relay((0, 1, 3, 0), "m")
    landed((0, 1, 1, 0)), relay((0, 1, 1, 0), "l", 1), relay((0, 1, 1, 0), "m")
    landed((0, 0, 2, 0)), relay((0, 0, 2, 0), "m")
    multiply(0, 0, 1)
    multiply(0, 1, 0)
    multiply(0, 0, 2)
    for slot in ((0, 3), (0, 1), (1, 0)):
        landed((1, *slot, 0)), landed((1, *slot, 1))
        multiply(1, *slot)
    landed((0, 1, 1, 1)), relay((0, 1, 1, 1), "m")
    landed((0, 1, 3, 1)), relay((0, 1, 3, 1), "m")
    multiply(0, 1, 1)
    multiply(0, 1, 3)
    landed((1, 0, 2, 0)), landed((1, 0, 2, 1))
    multiply(1, 0, 2)
    landed((0, 1, 2, 0), 0), landed((0, 1, 2, 0), 1), relay((0, 1, 2, 0), "m")
    landed((0, 1, 2, 1)), relay((0, 1, 2, 1), "m")
    multiply(0, 1, 2)
    for slot in ((1, 1), (1, 3), (1, 2)):
        landed((1, *slot, 0)), landed((1, *slot, 1))
        multiply(1, *slot)

    hid_n = {}
    for side, dy in ((0, 0), (1, 0), (0, 1), (1, 1)):
        g = accg[side, dy]
        hid[0, side, dy] = (g / (1.0 + jnp.exp(-g)) * accu[side, dy]).astype(BF16)
        n = hid_n[1 - side, dy] = sems.take()
        push(hid.at[0, side, dy], hid.at[1, 1 - side, dy], n, mate)
    loads[2].wait()
    wd_move.wait()
    for (side, dy), n in hid_n.items():
        arrive(hid.at[1, side, dy], n)

    def down(dy, dx):
        columns = pl.ds(pl.multiple_of(lax.rem(x + dx, 4) * HALF, HALF), HALF)
        for i in range(2):
            yb[dy, dx, i] = (
                dot(hid[0, i, dy], wd[0, :, columns]) + dot(hid[1, i, dy], wd[1, :, columns])
            ).astype(BF16)

    def add(into, *terms):
        value = into[...].astype(F32)
        for ref, _ in terms:
            value += ref[...].astype(F32)
        into[...] = value.astype(BF16)

    def give(src, dst, device):
        n = sems.take()
        push(src, dst, n, device)
        return dst, n

    def wait_all(*terms):
        for ref, n in terms:
            arrive(ref, n)

    down(1, 2)
    from_y2 = give(yb.at[1, 2, 1], rh.at[0], across)
    from_r_q = give(yb.at[1, 2, 0, pl.ds(0, QUARTER)], rq.at[0], left)
    from_l_q = give(yb.at[1, 2, 0, pl.ds(QUARTER, QUARTER)], rq.at[1], right)
    down(0, 2)
    from_r_2 = give(yb.at[0, 2, 0], rh.at[1], left)
    down(1, 3)
    from_y_3 = give(yb.at[1, 3, 1], rh.at[2], across)
    down(1, 1)
    from_y_1 = give(yb.at[1, 1, 1], rh.at[3], across)
    wait_all(from_y2, from_r_q, from_l_q)
    add(yb.at[0, 2, 1], from_y2)
    from_l_2 = give(yb.at[0, 2, 1], rh.at[4], right)
    add(yb.at[1, 3, 0, pl.ds(0, QUARTER)], from_r_q)
    from_r_3 = give(yb.at[1, 3, 0], rh.at[5], left)
    add(yb.at[1, 1, 0, pl.ds(QUARTER, QUARTER)], from_l_q)
    from_l_1 = give(yb.at[1, 1, 0], rh.at[6], right)
    down(0, 1)
    last_l = [give(yb.at[0, 1, 0], rf.at[0, 0], right), None]
    down(1, 0)
    last_y = [None, give(yb.at[1, 0, 1], rf.at[1, 1], across)]
    down(0, 3)
    wait_all(from_r_2)
    add(yb.at[0, 3, 0], from_r_2)
    last_r = [give(yb.at[0, 3, 0], rf.at[2, 0], left), None]
    wait_all(from_y_3)
    add(yb.at[0, 3, 1], from_y_3)
    last_r[1] = give(yb.at[0, 3, 1], rf.at[2, 1], left)
    wait_all(from_y_1, from_l_2)
    add(yb.at[0, 1, 1], from_y_1, from_l_2)
    last_l[1] = give(yb.at[0, 1, 1], rf.at[0, 1], right)
    wait_all(from_r_3, from_l_1)
    add(yb.at[1, 0, 0], from_r_3, from_l_1)
    last_y[0] = give(yb.at[1, 0, 0], rf.at[1, 0], across)
    down(0, 0)

    wide = lax.broadcasted_iota(jnp.int32, (8 * SLOT, ROWS), 0)
    tight = lax.broadcasted_iota(jnp.int32, (8 * SLOT, ROWS), 1)
    block = sum([jnp.where(tight >= CAP * i, 1, 0) for i in range(1, 8)])
    spread = jnp.where(wide == tight + block * (SLOT - CAP), 1.0, 0.0).astype(BF16)
    r2_n = sems.take(16)
    r2_s = sems.take(16)

    def back(i, r):
        s = lax.rem(me8 + r, 8)
        device = at(
            zl_=lax.div(s, 2),
            yh_=lax.rem(s, 2),
            core_=core if i == 0 else 1 - core,
            zh_=core,
        )
        return pltpu.make_async_remote_copy(
            src_ref=r2s.at[i, s], dst_ref=r2.at[zh, me8],
            send_sem=send.at[r2_s + 8 * i + r], recv_sem=recv.at[r2_n + zh * 8 + me8],
            device_id=device, device_id_type=MESH,
        )

    for i in range(2):
        wait_all(last_l[i], last_r[i], last_y[i])
        value = (
            yb[0, 0, i].astype(F32)
            + rf[0, i].astype(F32)
            + rf[1, i].astype(F32)
            + rf[2, i].astype(F32)
        ).astype(BF16)
        r2s[i] = dot(spread, value).astype(BF16).reshape(8, SLOT, HALF)
        if i == 0:

            @pl.when(core == zh)
            def _():
                r2[zh, me8] = r2s[0, me8]

            @pl.when(core != zh)
            def _():
                back(0, 0).start()

            pl.loop(1, 8)(lambda r: back(0, r).start())
        else:
            pl.loop(0, 8)(lambda r: back(1, r).start())

    @pl.loop(1, 16)
    def _(r):
        j = lax.rem(mine + r, 16)
        arrive(r2.at[lax.div(j, 8), lax.rem(j, 8)], r2_n + j)

    @pl.when(core != zh)
    def _():
        arrive(r2.at[zh, me8], r2_n + mine)

    mix = stream[...]
    for i in range(2):
        back_rows = r2[i].reshape(8 * SLOT, HALF)
        mix += dot(cw[0], back_rows) + dot(cw[1], back_rows)
    out_ref[...] = mix.astype(BF16)

    for src, n in started:
        copy(src, src, n, mate).wait_send()

    @pl.loop(1, 16)
    def _(r):
        copy(kv.at[0, 0], kv.at[0, 0], kv_n + r, mate).wait_send()
        copy(gbuf.at[0], gbuf.at[0], d1_n + r, mate).wait_send()

    @pl.loop(0, 16)
    def _(r):
        copy(kv.at[0, 0], kv.at[0, 0], mate_n + r, mate).wait_send()

    @pl.loop(1, 8)
    def _(r):
        copy(ssq.at[0], ssq.at[0], ssq_n + r, mate).wait_send()

    @pl.when(core != zh)
    def _():
        back(0, 0).wait_send()

    pl.loop(1, 8)(lambda r: back(0, r).wait_send())
    pl.loop(0, 8)(lambda r: back(1, r).wait_send())
    print("semaphores", sems.used) if False else None


SEMS = 192


def body(
    query_rows, key_head_rows, value_head_rows, positions, residual, norm_gain, expert_ids,
    gate_fixed, w_gate, w_up, w_down,
):
    ints = jnp.concatenate([expert_ids, gate_fixed[:, None], positions[:, None]], axis=1)
    vmem = pl.BlockSpec(memory_space=pltpu.VMEM)
    hbm = pl.BlockSpec(memory_space=pl.ANY)
    return pl.pallas_call(
        kernel,
        out_shape=jax.ShapeDtypeStruct(residual.shape, BF16),
        in_specs=[vmem] * 7 + [hbm] * 3,
        out_specs=vmem,
        scratch_shapes=[
            pltpu.VMEM((2, 16, 272, 128), BF16),
            pltpu.VMEM((8, 8, 128), F32),
            pltpu.VMEM((128, HALF), F32),
            pltpu.VMEM((128, EXPERTS * SLOT), BF16),
            pltpu.VMEM((2, 128, EXPERTS * SLOT), BF16),
            pltpu.VMEM((EXPERTS, SLOT, HALF), BF16),
            pltpu.VMEM((2, 8, SLOT, HALF), BF16),
            pltpu.VMEM((2, 2, 4, 2, ROWS, HALF), BF16),
            pltpu.VMEM(w_gate.shape, BF16),
            pltpu.VMEM(w_up.shape, BF16),
            pltpu.VMEM((2, w_down.shape[0], 2048), BF16),
            pltpu.VMEM((2, 2, ROWS, w_gate.shape[1]), F32),
            pltpu.VMEM((2, 2, ROWS, w_gate.shape[1]), F32),
            pltpu.VMEM((2, 2, 2, ROWS, w_gate.shape[1]), BF16),
            pltpu.VMEM((2, 4, 2, ROWS, HALF), BF16),
            pltpu.VMEM((2, QUARTER, HALF), BF16),
            pltpu.VMEM((7, ROWS, HALF), BF16),
            pltpu.VMEM((3, 2, ROWS, HALF), BF16),
            pltpu.VMEM((8, 128), F32),
            pltpu.VMEM((2, 8, SLOT, HALF), BF16),
            pltpu.VMEM((2, 8, SLOT, HALF), BF16),
            pltpu.SemaphoreType.DMA((SEMS,)),
            pltpu.SemaphoreType.DMA((SEMS,)),
            pltpu.SemaphoreType.DMA((3,)),
        ],
        compiler_params=pltpu.CompilerParams(
            collective_id=0, has_side_effects=True, vmem_limit_bytes=60 * 2**20
        ),
        cost_estimate=pl.CostEstimate(
            flops=14 * 10**9, bytes_accessed=12 * 10**6, transcendentals=3 * 10**6
        ),
    )(
        query_rows, key_head_rows, value_head_rows, ints, positions.reshape(1, -1), residual,
        norm_gain.reshape(1, -1), w_gate, w_up, w_down,
    )


def solution(mesh):
    in_specs = (
        P("ctx", "head"),
        P("ctx", "head"),
        P("ctx", "head"),
        P("ctx"),
        P("ctx", "head"),
        P("head"),
        P("ctx", None),
        P("ctx"),
        P(None, ("ctx", "head")),
        P(None, ("ctx", "head")),
        P(("ctx", "head"), None),
    )
    out_specs = P("ctx", "head")
    return jax.shard_map(body, mesh=mesh, in_specs=in_specs, out_specs=out_specs, check_vma=False)
```

time: 790 us -> 184 us (0.23)
  waiting for transfers between devices: 384 us -> 0 us
  blocking collectives: 309 us -> 0 us
  Pallas kernels: 0 us -> 165 us
  matrix products: 38.4 us -> 0 us
  local copies, waits for them, and re-layouts: 32.2 us -> 16.5 us
  between operations: 13.3 us -> 0.01 us
    all_to_all x1 -> x0, blocking collectives: 237 us -> none  [body(): lax.all_to_all(copies.reshape(ctx_count, CAP, piece_width), 'ctx', split_...]
    reduce_scatter x1 -> x0, waiting for transfers between devices: 197 us -> none  [body(): lax.psum_scatter(down_terms.astype(jnp.bfloat16), 'head', scatter_dimensi...]
    pallas_call x0 -> x1, Pallas kernels: none -> 165 us  [body(): pl.pallas_call(kernel, out_shape=jax.ShapeDtypeStruct(residual.shape, BF1...]
    all_gather x4 -> x0, waiting for transfers between devices: 153 us -> none  [the longest x1 59.7 us: body(): lax.all_gather(attention, 'head', axis=1, tiled=True)]
    all_gather x2 -> x0, blocking collectives: 72.6 us -> none  [the longest x1 37.4 us: body(): p_piece = lax.all_gather(positions, 'ctx', axis=0, tiled=True)]
    dot_general x6 -> x0, matrix products: 38.4 us -> none  [the longest x1 17.4 us: body(): down_terms = jnp.dot(hidden, w_down, preferred_element_type=jnp.float32)]
    all_to_all x1 -> x0, waiting for transfers between devices: 32.2 us -> none  [body(): lax.all_to_all(shares.reshape(ctx_count, CAP, -1).astype(jnp.bfloat16), '...]
    reshape x4 -> x1, local copies, waits for them, and re-layouts: 13.5 us -> 1.25 us  [body(): norm_gain.reshape(1, -1)]
  transfers between devices with their start and end apart: 6 -> 0, of which waited for: 6 -> 0; matrix products, arithmetic and copies ran while one was open for 2% -> 0% of each run, Pallas kernels for 0% -> 0%
where the time goes in v1:
time: 184 us; the launch traced here: 182 us
  Pallas kernels  165 us (90%)
  local copies, waits for them, and re-layouts  16.5 us (9%)
    pallas_call x1, Pallas kernels, body(): pl.pallas_call(kernel, out_shape=jax.ShapeDtypeStruct(residual.shape, BF1...  165 us
    unnamed x3, local copies, waits for them, and re-layouts  14.5 us

profile of v1, /device:TPU:33, one launch (start us, length us, event | category | flops | bytes accessed | tf_op | source)
XLA Modules:
  0.0 182.5 jit_solution(6994665944779453674)
XLA Ops:
  0.0 1.3 reshape.7.gain_ref
  1.3 0.7 pad_add_fusion
  2.0 0.7 copy.17.ints_ref
  2.7 6.4 %copy.18.wg_hbm = bf16[4096,448]{1,0:T(8,128)(2,1)} copy(bf16[4096,448]{0,1:T(8,128)(2,1)} %param.19) | data formatting | bytes 7340032 | tf_op args[8]
  9.1 6.5 %copy.19.wu_hbm = bf16[4096,448]{1,0:T(8,128)(2,1)} copy(bf16[4096,448]{0,1:T(8,128)(2,1)} %param.20) | data formatting | bytes 7340032 | tf_op args[9]
  15.6 165.3 %shard_map.109 = bf16[128,512]{1,0:T(8,128)(2,1)} custom-call(bf16[128,512]{1,0:T(8,128)(2,1)} %q_ref.1, bf16[128,128]{1,0:T(8,128)(2,1)} %k_ref.1, bf16[128,128]{1,0:T(8,128)(2,1)} %v_ref.1, s32[128,4]{1,0:T(8,128)} %copy.17.ints_ref, s32[1,128]{1,0:T(1,128)} %bitcast.5, bf16[128,512]{1,0:T(8,128)(2,1)} %resid_ref.1, bf16[1,512]{1,0:T(2,128)(2,1)} %reshape.7.gain_ref, ...), custom_call_target="tpu_custom_call" | custom-call | flops 14000000000 | bytes 12000000 | tf_op jit(solution)/shard_map/pallas_call | solution.py:475
  180.9 1.6 copy.21

commit v2 on v1

--- a/solution.py
+++ b/solution.py
@@ -32,10 +32,14 @@
     return jnp.dot(a, b, preferred_element_type=F32)
 
 
+def dot_t(a, b):
+    return lax.dot_general(a, b, (((1,), (1,)), ((), ())), preferred_element_type=F32)
+
+
 def kernel(
-    q_ref, k_ref, v_ref, ints_ref, posrow_ref, resid_ref, gain_ref, wg_hbm, wu_hbm, wd_hbm,
+    q_ref, k_ref, v_ref, ids_ref, gate_ref, pos_ref, resid_ref, gain_ref, wg_hbm, wu_hbm, wd_hbm,
     out_ref,
-    kv, ssq, stream, pick, cw, gbuf, d1, xb, wg, wu, wd, accg, accu, hid, yb, rq, rh, rf, z, r2s, r2,
+    kv, ssq, stream, pick, cw, gbuf, d1, xb, wg, wu, wd, accg, accu, hid, yb, rq, rh, rf, r2s, r2,
     send, recv, local,
 ):
     c, h = lax.axis_index("ctx"), lax.axis_index("head")
@@ -46,8 +50,14 @@
     def at(zl_=zl, yh_=yh, yl_=yl, core_=core, zh_=zh, x_=x):
         return (zl_ * 8 + (yh_ * 2 + yl_) * 2 + core_, zh_ * 4 + x_)
 
+    def kin(zl_=zl, yh_=yh, core_=core, zh_=zh):
+        return at(zl_=zl_, yh_=yh_, yl_=lax.rem(yl + yh + yh_, 2), core_=core_, zh_=zh_)
+
     right, left = at(x_=lax.rem(x + 1, 4)), at(x_=lax.rem(x + 3, 4))
     across, mate = at(yl_=1 - yl), at(core_=1 - core)
+    up, under = (
+        at(yh_=lax.div(lax.rem(y + i, 4), 2), yl_=lax.rem(y + i, 2)) for i in (1, 3)
+    )
     sems = Sems(send, recv)
 
     def copy(src, dst, n, device):
@@ -75,29 +85,20 @@
     for load in loads:
         load.start()
 
-    kv[0, 0, 0:128, :] = k_ref[...]
-    kv[0, 0, 128:256, :] = v_ref[...]
-    pos = posrow_ref[...]
+    kv[0, 0, 0, 0:128, :] = k_ref[...]
+    kv[0, 0, 0, 128:256, :] = v_ref[...]
+    pos = pos_ref[...]
     pos_hi = lax.shift_right_logical(pos, 6).astype(F32)
     pos_lo = (pos & 63).astype(F32)
     row16 = lax.broadcasted_iota(jnp.int32, (16, 128), 0)
-    kv[0, 0, 256:272, :] = jnp.where(row16 == 0, pos_hi, pos_lo).astype(BF16)
+    kv[0, 0, 0, 256:272, :] = jnp.where(row16 == 0, pos_hi, pos_lo).astype(BF16)
 
     barrier = pltpu.get_barrier_semaphore()
-    me16 = zl * 4 + y
     me32 = ((zh * 4 + zl) * 2 + yh) * 2 + core
 
     def greet(device):
         pl.semaphore_signal(barrier, inc=1, device_id=device, device_id_type=MESH)
 
-    def kv_peer(r):
-        j = lax.rem(me16 + r, 16)
-        return (lax.div(j, 4) * 8 + lax.rem(j, 4) * 2 + core, h)
-
-    @pl.loop(1, 16)
-    def _(r):
-        greet(kv_peer(r))
-
     @pl.loop(1, 8)
     def _(r):
         greet((c, lax.rem(h + r, 8)))
@@ -106,7 +107,7 @@
     def _(r):
         j = lax.rem(me32 + r, 32)
         greet(
-            at(
+            kin(
                 zl_=lax.rem(lax.div(j, 4), 4),
                 yh_=lax.rem(lax.div(j, 2), 2),
                 core_=lax.rem(j, 2),
@@ -114,49 +115,61 @@
             )
         )
 
-    pl.semaphore_wait(barrier, 15 + 7 + 31)
-
-    kv_n, mate_n, wd_n = sems.take(16), sems.take(16), sems.take()
-
-    @pl.loop(1, 16)
-    def _(r):
-        copy(kv.at[0, 0], kv.at[0, r], kv_n + r, kv_peer(r)).start()
-
-    copy(kv.at[0, 0], kv.at[1, 0], mate_n, mate).start()
+    greet(up), greet(under)
+    pl.semaphore_wait(barrier, 7 + 31 + 2)
+
+    kv_n, kv_half, mate_n, wd_n = sems.take(16), sems.take(4), sems.take(16), sems.take()
+
+    def kv_mate(dy, dz):
+        n = mate_n + dy * 4 + dz
+        copy(kv.at[0, dy, dz], kv.at[1, dy, dz], n, mate).start()
+
+    def kv_round(dz):
+        copy(kv.at[0, 0, dz], kv.at[0, 3, dz], kv_n + 12 + dz, up).start()
+        copy(kv.at[0, 0, dz], kv.at[0, 1, dz], kv_n + 4 + dz, under).start()
+
+    for dz in (3, 1, 2):
+        copy(kv.at[0, 0, 0], kv.at[0, 0, dz], kv_n + dz, at(zl_=lax.rem(zl + 4 - dz, 4))).start()
+    kv_round(0)
+    kv_mate(0, 0)
     other = pl.multiple_of((1 - core) * 2048, 128)
     wd_move = copy(wd_hbm.at[:, pl.ds(other, 2048)], wd.at[1], wd_n, mate)
     wd_move.start()
 
-    ids0, ids1 = ints_ref[:, 0:1], ints_ref[:, 1:2]
+    numbers = jnp.concatenate(
+        [ids_ref[...].astype(F32), gate_ref[...].astype(F32), pos.astype(F32)] * 32, axis=0
+    )
+    numbers = jnp.transpose(numbers)
+    ids0, ids1, gates, places = (numbers[:, i : i + 1] for i in range(4))
     lane = lax.broadcasted_iota(jnp.int32, (128, 128), 1)
     below = lax.broadcasted_iota(jnp.int32, (128, 128), 0) > lane
-    hit0, hit1 = lane == ids0, lane == ids1
+    hit0, hit1 = lane.astype(F32) == ids0, lane.astype(F32) == ids1
     hits = jnp.where(hit0 | hit1, 1.0, 0.0).astype(BF16)
     ranks = dot(jnp.where(below, 1.0, 0.0).astype(BF16), hits)
-    slot0 = ids0.astype(F32) * SLOT + jnp.sum(jnp.where(hit0, ranks, 0.0), axis=1, keepdims=True)
-    slot1 = ids1.astype(F32) * SLOT + jnp.sum(jnp.where(hit1, ranks, 0.0), axis=1, keepdims=True)
-    places = lax.broadcasted_iota(jnp.int32, (128, EXPERTS * SLOT), 1).astype(F32)
-    at0, at1 = places == slot0, places == slot1
+    slot0 = ids0 * SLOT + jnp.sum(jnp.where(hit0, ranks, 0.0), axis=1, keepdims=True)
+    slot1 = ids1 * SLOT + jnp.sum(jnp.where(hit1, ranks, 0.0), axis=1, keepdims=True)
+    slots = lax.broadcasted_iota(jnp.int32, (128, EXPERTS * SLOT), 1).astype(F32)
+    at0, at1 = slots == slot0, slots == slot1
     pick[...] = jnp.where(at0 | at1, 1.0, 0.0).astype(BF16)
-    first = ints_ref[:, 2:3].astype(F32) / 65536.0
+    first = gates / 65536.0
     weights = jnp.where(at0, first, 0.0) + jnp.where(at1, 1.0 - first, 0.0)
     coarse = weights.astype(BF16)
     cw[0] = coarse
     cw[1] = (weights - coarse.astype(F32)).astype(BF16)
 
     q = jnp.concatenate([q_ref[:, 128 * i : 128 * i + 128] for i in range(4)], axis=0)
-    q_pos = jnp.concatenate([ints_ref[:, 3:4].astype(F32)] * 4, axis=0)
+    q_pos = jnp.concatenate([places] * 4, axis=0)
 
     def attend(side, group, carry):
         top, total, acc = carry
-        part = kv[side, pl.ds(group * 4, 4)]
+        part = kv[side, group]
         keys = part[:, 0:128, :].reshape(512, 128)
         values = part[:, 128:256, :].reshape(512, 128)
-        places = part[:, 256:272, :].astype(F32)
+        digits = part[:, 256:272, :].astype(F32)
         k_pos = jnp.concatenate(
-            [places[i, 0:1, :] * 64.0 + places[i, 1:2, :] for i in range(4)], axis=1
+            [digits[i, 0:1, :] * 64.0 + digits[i, 1:2, :] for i in range(4)], axis=1
         )
-        scores = lax.dot_general(q, keys, (((1,), (1,)), ((), ())), preferred_element_type=F32)
+        scores = dot_t(q, keys)
         scores = jnp.where(k_pos <= q_pos, scores * SCALE, -1e30)
         new_top = jnp.maximum(top, jnp.max(scores, axis=1, keepdims=True))
         keep = jnp.exp(top - new_top)
@@ -165,25 +178,34 @@
         acc = acc * keep + dot(probs.astype(BF16), values)
         return new_top, total, acc
 
-    def own_side(group, carry):
-        for i in range(4):
-            r = group * 4 + i
-
-            @pl.when(r > 0)
-            def _(r=r):
-                arrive(kv.at[0, r], kv_n + r)
-                copy(kv.at[0, r], kv.at[1, r], mate_n + r, mate).start()
-
-        return attend(0, group, carry)
-
-    def mate_side(group, carry):
-        for i in range(4):
-            r = group * 4 + i
-            arrive(kv.at[1, r], mate_n + r)
-        return attend(1, group, carry)
+    early, late = pl.ds(0, 128), pl.ds(128, 144)
+
+    def mate_side(step, carry):
+        dy = step ^ lax.shift_right_logical(step, 1)
+        for dz in range(4):
+            arrive(kv.at[1, dy, dz], mate_n + dy * 4 + dz)
+        return attend(1, dy, carry)
 
     carry = (jnp.full((512, 1), -1e30, F32), jnp.zeros((512, 1), F32), jnp.zeros((512, 128), F32))
-    carry = lax.fori_loop(0, 4, own_side, carry)
+    for dz in (1, 3, 2):
+        arrive(kv.at[0, 0, dz], kv_n + dz)
+        kv_round(dz)
+        kv_mate(0, dz)
+    carry = attend(0, 0, carry)
+    for dz in (0, 1, 3, 2):
+        arrive(kv.at[0, 3, dz], kv_n + 12 + dz)
+        copy(kv.at[0, 3, dz, early], kv.at[0, 2, dz, early], kv_n + 8 + dz, up).start()
+        kv_mate(3, dz)
+        arrive(kv.at[0, 1, dz], kv_n + 4 + dz)
+        copy(kv.at[0, 1, dz, late], kv.at[0, 2, dz, late], kv_half + dz, under).start()
+        kv_mate(1, dz)
+    carry = attend(0, 1, carry)
+    carry = attend(0, 3, carry)
+    for dz in (0, 1, 3, 2):
+        arrive(kv.at[0, 2, dz, early], kv_n + 8 + dz)
+        arrive(kv.at[0, 2, dz, late], kv_half + dz)
+        kv_mate(2, dz)
+    carry = attend(0, 2, carry)
     _, total, acc = lax.fori_loop(0, 4, mate_side, carry)
     att = (acc / total).astype(BF16).astype(F32)
     att = jnp.concatenate([att[128 * i : 128 * i + 128] for i in range(4)], axis=1)
@@ -214,25 +236,24 @@
     me8 = zl * 2 + yh
     mine = zh * 8 + me8
 
-    @pl.loop(1, 16)
-    def _(r):
-        j = lax.rem(mine + r, 16)
-        e = lax.rem(j, 8)
-        device = at(zl_=lax.div(e, 2), yh_=lax.rem(e, 2), zh_=lax.div(j, 8))
-        copy(gbuf.at[e], d1.at[zh, me8], d1_n + r, device).start()
-
-    d1[zh, me8] = gbuf[me8]
-
-    @pl.loop(1, 16)
-    def _(r):
-        j = lax.rem(mine + 16 - r, 16)
-        arrive(d1.at[lax.div(j, 8), lax.rem(j, 8)], d1_n + r)
+    def dispatch(i, r):
+        e = lax.rem(me8 + r, 8)
+        device = kin(zl_=lax.div(e, 2), yh_=lax.rem(e, 2), zh_=zh if i == 0 else 1 - zh)
+        copy(gbuf.at[e], d1.at[i, me8], d1_n + 8 * i + r, device).start()
+
+    pl.loop(1, 8)(lambda r: dispatch(0, r))
+    pl.loop(0, 8)(lambda r: dispatch(1, r))
+    d1[0, me8] = gbuf[me8]
+
+    def dispatched(i, r):
+        arrive(d1.at[i, lax.rem(me8 + 8 - r, 8)], d1_n + 8 * i + r)
 
     tight = lax.broadcasted_iota(jnp.int32, (ROWS, 8 * SLOT), 0)
     wide = lax.broadcasted_iota(jnp.int32, (ROWS, 8 * SLOT), 1)
     block = sum([jnp.where(tight >= CAP * i, 1, 0) for i in range(1, 8)])
     compact = jnp.where(wide == tight + block * (SLOT - CAP), 1.0, 0.0).astype(BF16)
-    for i in range(2):
+
+    def compacted(i):
         xb[0, 0, 0, i] = dot(compact, d1[i].reshape(8 * SLOT, HALF)).astype(BF16)
 
     got = {}
@@ -257,27 +278,29 @@
         there, n = got[(*slot, rows_of)]
         arrive(there, n)
 
+    def multiply(side, dy, dx):
+        xs = lax.rem(x + dx, 4)
+        low = pl.ds(pl.multiple_of((zh * 4 + xs) * HALF, HALF), HALF)
+        high = pl.ds(pl.multiple_of(((1 - zh) * 4 + xs) * HALF, HALF), HALF)
+        a, b = xb[side, dy, dx, 0], xb[side, dy, dx, 1]
+        accg[side, dy] += dot_t(a, wg[:, low]) + dot_t(b, wg[:, high])
+        accu[side, dy] += dot_t(a, wu[:, low]) + dot_t(b, wu[:, high])
+
+    own = [(0, 0, 0, 0), (0, 0, 0, 1)]
+    pl.loop(1, 8)(lambda r: dispatched(0, r))
+    compacted(0)
+    relay(own[0], "r"), relay(own[0], "l"), relay(own[0], "y"), relay(own[0], "m")
     for load in loads[:2]:
         load.wait()
     accg[...] = jnp.zeros_like(accg)
     accu[...] = jnp.zeros_like(accu)
-
-    def multiply(side, dy, dx):
-        xs = lax.rem(x + dx, 4)
-        low = pl.ds(pl.multiple_of(xs * HALF, HALF), HALF)
-        high = pl.ds(pl.multiple_of(2048 + xs * HALF, HALF), HALF)
-        a, b = xb[side, dy, dx, 0], xb[side, dy, dx, 1]
-        accg[side, dy] += dot(a, wg[low, :]) + dot(b, wg[high, :])
-        accu[side, dy] += dot(a, wu[low, :]) + dot(b, wu[high, :])
-
-    own = [(0, 0, 0, 0), (0, 0, 0, 1)]
-    relay(own[0], "r"), relay(own[1], "l"), relay(own[0], "y")
-    relay(own[1], "r"), relay(own[0], "l"), relay(own[1], "y")
-    relay(own[0], "m"), relay(own[1], "m")
+    pl.loop(0, 8)(lambda r: dispatched(1, r))
+    compacted(1)
+    relay(own[1], "l"), relay(own[1], "r"), relay(own[1], "y"), relay(own[1], "m")
+    landed((0, 0, 3, 0)), relay((0, 0, 3, 0), "r")
+    landed((0, 1, 0, 0)), relay((0, 1, 0, 0), "r"), relay((0, 1, 0, 0), "l")
     multiply(0, 0, 0)
-    landed((0, 0, 3, 0)), relay((0, 0, 3, 0), "r")
     landed((0, 0, 1, 1)), relay((0, 0, 1, 1), "l"), relay((0, 0, 1, 1), "y")
-    landed((0, 1, 0, 0)), relay((0, 1, 0, 0), "r"), relay((0, 1, 0, 0), "l")
     landed((0, 0, 3, 1)), relay((0, 0, 3, 1), "y")
     landed((0, 0, 1, 0)), landed((0, 1, 0, 1))
     for slot in ((0, 3), (0, 1), (1, 0)):
@@ -387,11 +410,8 @@
 
     def back(i, r):
         s = lax.rem(me8 + r, 8)
-        device = at(
-            zl_=lax.div(s, 2),
-            yh_=lax.rem(s, 2),
-            core_=core if i == 0 else 1 - core,
-            zh_=core,
+        device = kin(
+            zl_=lax.div(s, 2), yh_=lax.rem(s, 2), core_=core if i == 0 else 1 - core, zh_=core
         )
         return pltpu.make_async_remote_copy(
             src_ref=r2s.at[i, s], dst_ref=r2.at[zh, me8],
@@ -442,12 +462,17 @@
 
     @pl.loop(1, 16)
     def _(r):
-        copy(kv.at[0, 0], kv.at[0, 0], kv_n + r, mate).wait_send()
         copy(gbuf.at[0], gbuf.at[0], d1_n + r, mate).wait_send()
 
     @pl.loop(0, 16)
     def _(r):
-        copy(kv.at[0, 0], kv.at[0, 0], mate_n + r, mate).wait_send()
+        copy(kv.at[0, 0, 0], kv.at[0, 0, 0], mate_n + r, mate).wait_send()
+
+    for n in (*range(1, 8), *range(12, 16)):
+        copy(kv.at[0, 0, 0], kv.at[0, 0, 0], kv_n + n, mate).wait_send()
+    for n in range(4):
+        copy(kv.at[0, 0, 0, early], kv.at[0, 0, 0, early], kv_n + 8 + n, mate).wait_send()
+        copy(kv.at[0, 0, 0, late], kv.at[0, 0, 0, late], kv_half + n, mate).wait_send()
 
     @pl.loop(1, 8)
     def _(r):
@@ -459,7 +484,6 @@
 
     pl.loop(1, 8)(lambda r: back(0, r).wait_send())
     pl.loop(0, 8)(lambda r: back(1, r).wait_send())
-    print("semaphores", sems.used) if False else None
 
 
 SEMS = 192
@@ -469,16 +493,15 @@
     query_rows, key_head_rows, value_head_rows, positions, residual, norm_gain, expert_ids,
     gate_fixed, w_gate, w_up, w_down,
 ):
-    ints = jnp.concatenate([expert_ids, gate_fixed[:, None], positions[:, None]], axis=1)
     vmem = pl.BlockSpec(memory_space=pltpu.VMEM)
     hbm = pl.BlockSpec(memory_space=pl.ANY)
     return pl.pallas_call(
         kernel,
         out_shape=jax.ShapeDtypeStruct(residual.shape, BF16),
-        in_specs=[vmem] * 7 + [hbm] * 3,
+        in_specs=[vmem] * 8 + [hbm] * 3,
         out_specs=vmem,
         scratch_shapes=[
-            pltpu.VMEM((2, 16, 272, 128), BF16),
+            pltpu.VMEM((2, 4, 4, 272, 128), BF16),
             pltpu.VMEM((8, 8, 128), F32),
             pltpu.VMEM((128, HALF), F32),
             pltpu.VMEM((128, EXPERTS * SLOT), BF16),
@@ -486,8 +509,8 @@
             pltpu.VMEM((EXPERTS, SLOT, HALF), BF16),
             pltpu.VMEM((2, 8, SLOT, HALF), BF16),
             pltpu.VMEM((2, 2, 4, 2, ROWS, HALF), BF16),
-            pltpu.VMEM(w_gate.shape, BF16),
-            pltpu.VMEM(w_up.shape, BF16),
+            pltpu.VMEM(w_gate.shape[::-1], BF16),
+            pltpu.VMEM(w_up.shape[::-1], BF16),
             pltpu.VMEM((2, w_down.shape[0], 2048), BF16),
             pltpu.VMEM((2, 2, ROWS, w_gate.shape[1]), F32),
             pltpu.VMEM((2, 2, ROWS, w_gate.shape[1]), F32),
@@ -496,7 +519,6 @@
             pltpu.VMEM((2, QUARTER, HALF), BF16),
             pltpu.VMEM((7, ROWS, HALF), BF16),
             pltpu.VMEM((3, 2, ROWS, HALF), BF16),
-            pltpu.VMEM((8, 128), F32),
             pltpu.VMEM((2, 8, SLOT, HALF), BF16),
             pltpu.VMEM((2, 8, SLOT, HALF), BF16),
             pltpu.SemaphoreType.DMA((SEMS,)),
@@ -510,8 +532,8 @@
             flops=14 * 10**9, bytes_accessed=12 * 10**6, transcendentals=3 * 10**6
         ),
     )(
-        query_rows, key_head_rows, value_head_rows, ints, positions.reshape(1, -1), residual,
-        norm_gain.reshape(1, -1), w_gate, w_up, w_down,
+        query_rows, key_head_rows, value_head_rows, expert_ids.T, gate_fixed.reshape(1, -1),
+        positions.reshape(1, -1), residual, norm_gain.reshape(1, -1), w_gate.T, w_up.T, w_down,
     )
 
 

time: 184 us -> 154 us (0.84)
  Pallas kernels: 165 us -> 151 us
  local copies, waits for them, and re-layouts: 16.5 us -> 2.83 us
    pallas_call x1, Pallas kernels: 165 us -> 151 us  [body(): pl.pallas_call(kernel, out_shape=jax.ShapeDtypeStruct(residual.shape, BF1...]
    unnamed x3 -> x1, local copies, waits for them, and re-layouts: 14.5 us -> 1.57 us
where the time goes in v2:
time: 154 us
  Pallas kernels  151 us (98%)
  local copies, waits for them, and re-layouts  2.83 us (2%)
    pallas_call x1, Pallas kernels, body(): pl.pallas_call(kernel, out_shape=jax.ShapeDtypeStruct(residual.shape, BF1...  151 us

profile of v2, /device:TPU:33, one launch (start us, length us, event | category | flops | bytes accessed | tf_op | source)
XLA Modules:
  0.0 154.0 jit_solution(120793728699602321)
XLA Ops:
  0.0 1.3 reshape.11.gain_ref
  1.3 151.2 %shard_map.109 = bf16[128,512]{1,0:T(8,128)(2,1)} custom-call(bf16[128,512]{1,0:T(8,128)(2,1)} %q_ref.1, bf16[128,128]{1,0:T(8,128)(2,1)} %k_ref.1, bf16[128,128]{1,0:T(8,128)(2,1)} %v_ref.1, s32[2,128]{1,0:T(2,128)} %bitcast.7, s32[1,128]{1,0:T(1,128)} %bitcast.8, s32[1,128]{1,0:T(1,128)} %bitcast.9, bf16[128,512]{1,0:T(8,128)(2,1)} %resid_ref.1, ...), custom_call_target="tpu_custom_call" | custom-call | flops 14000000000 | bytes 12000000 | tf_op jit(solution)/shard_map/pallas_call | solution.py:498
  152.4 1.6 %copy.13 = bf16[128,512]{1,0:T(8,128)(2,1)} copy(bf16[128,512]{1,0:T(8,128)(2,1)} %shard_map.109) | data formatting | bytes 262144

commit v3 on v2

--- a/solution.py
+++ b/solution.py
@@ -8,7 +8,7 @@
 MESH = pl.DeviceIdType.MESH
 HEAD_SIZE = 128
 CAP = 36
-SLOT = 48
+PACK = 4 * CAP
 EXPERTS = 8
 ROWS = 8 * CAP
 HALF = 512
@@ -36,10 +36,14 @@
     return lax.dot_general(a, b, (((1,), (1,)), ((), ())), preferred_element_type=F32)
 
 
+def fold(a):
+    return jnp.concatenate([a[:, 128 * j : 128 * j + 128] for j in range(4)], axis=0)
+
+
 def kernel(
     q_ref, k_ref, v_ref, ids_ref, gate_ref, pos_ref, resid_ref, gain_ref, wg_hbm, wu_hbm, wd_hbm,
     out_ref,
-    kv, ssq, stream, pick, cw, gbuf, d1, xb, wg, wu, wd, accg, accu, hid, yb, rq, rh, rf, r2s, r2,
+    kv, ssq, stream, pick, cw, turn, gbuf, d1, xb, wg, wu, wd, accg, accu, hid, yb, rq, rh, rf, r2s, r2,
     send, recv, local,
 ):
     c, h = lax.axis_index("ctx"), lax.axis_index("head")
@@ -141,23 +145,8 @@
     )
     numbers = jnp.transpose(numbers)
     ids0, ids1, gates, places = (numbers[:, i : i + 1] for i in range(4))
-    lane = lax.broadcasted_iota(jnp.int32, (128, 128), 1)
-    below = lax.broadcasted_iota(jnp.int32, (128, 128), 0) > lane
-    hit0, hit1 = lane.astype(F32) == ids0, lane.astype(F32) == ids1
-    hits = jnp.where(hit0 | hit1, 1.0, 0.0).astype(BF16)
-    ranks = dot(jnp.where(below, 1.0, 0.0).astype(BF16), hits)
-    slot0 = ids0 * SLOT + jnp.sum(jnp.where(hit0, ranks, 0.0), axis=1, keepdims=True)
-    slot1 = ids1 * SLOT + jnp.sum(jnp.where(hit1, ranks, 0.0), axis=1, keepdims=True)
-    slots = lax.broadcasted_iota(jnp.int32, (128, EXPERTS * SLOT), 1).astype(F32)
-    at0, at1 = slots == slot0, slots == slot1
-    pick[...] = jnp.where(at0 | at1, 1.0, 0.0).astype(BF16)
-    first = gates / 65536.0
-    weights = jnp.where(at0, first, 0.0) + jnp.where(at1, 1.0 - first, 0.0)
-    coarse = weights.astype(BF16)
-    cw[0] = coarse
-    cw[1] = (weights - coarse.astype(F32)).astype(BF16)
-
-    q = jnp.concatenate([q_ref[:, 128 * i : 128 * i + 128] for i in range(4)], axis=0)
+
+    q = fold(q_ref[...])
     q_pos = jnp.concatenate([places] * 4, axis=0)
 
     def attend(side, group, carry):
@@ -220,6 +209,21 @@
     def _(r):
         copy(ssq.at[0], ssq.at[r], ssq_n + r, (c, lax.rem(h + r, 8))).start()
 
+    lane = lax.broadcasted_iota(jnp.int32, (128, 128), 1)
+    below = lax.broadcasted_iota(jnp.int32, (128, 128), 0) > lane
+    hit0, hit1 = lane.astype(F32) == ids0, lane.astype(F32) == ids1
+    hits = jnp.where(hit0 | hit1, 1.0, 0.0).astype(BF16)
+    ranks = dot(jnp.where(below, 1.0, 0.0).astype(BF16), hits)
+    slot0 = ids0 * PACK + jnp.sum(jnp.where(hit0, ranks, 0.0), axis=1, keepdims=True)
+    slot1 = ids1 * PACK + jnp.sum(jnp.where(hit1, ranks, 0.0), axis=1, keepdims=True)
+    row0, row1 = (
+        jnp.transpose(jnp.broadcast_to(slot, (128, 128)))[0:1, :] for slot in (slot0, slot1)
+    )
+    slots = lax.broadcasted_iota(jnp.int32, (EXPERTS * PACK, 128), 0).astype(F32)
+    for j in range(4):
+        hit = (slots == row0 + CAP * j) | (slots == row1 + CAP * j)
+        pick[:, 128 * j : 128 * j + 128] = jnp.where(hit, 1.0, 0.0).astype(BF16)
+
     @pl.loop(1, 8)
     def _(r):
         arrive(ssq.at[r], ssq_n + r)
@@ -227,14 +231,11 @@
     all_sq = jnp.sum(ssq[...], axis=0)
     all_sq = jnp.transpose(jnp.concatenate([all_sq] * 16, axis=0))[:, 0:1]
     normed = flow * lax.rsqrt(all_sq / 4096.0 + 1e-05) * gain_ref[...].astype(F32)
-    rows = lax.dot_general(
-        pick[...], normed.astype(BF16), (((0,), (0,)), ((), ())), preferred_element_type=F32
-    ).astype(BF16)
-    gbuf[...] = rows.reshape(EXPERTS, SLOT, HALF)
+    rows = dot(pick[...], fold(normed.astype(BF16)))
+    gbuf[...] = rows.astype(BF16).reshape(EXPERTS, PACK, 128)
 
     d1_n = sems.take(16)
     me8 = zl * 2 + yh
-    mine = zh * 8 + me8
 
     def dispatch(i, r):
         e = lax.rem(me8 + r, 8)
@@ -248,13 +249,19 @@
     def dispatched(i, r):
         arrive(d1.at[i, lax.rem(me8 + 8 - r, 8)], d1_n + 8 * i + r)
 
-    tight = lax.broadcasted_iota(jnp.int32, (ROWS, 8 * SLOT), 0)
-    wide = lax.broadcasted_iota(jnp.int32, (ROWS, 8 * SLOT), 1)
-    block = sum([jnp.where(tight >= CAP * i, 1, 0) for i in range(1, 8)])
-    compact = jnp.where(wide == tight + block * (SLOT - CAP), 1.0, 0.0).astype(BF16)
+    here = lax.broadcasted_iota(jnp.int32, (4 * PACK, 1), 0)
+    outer = sum([jnp.where(here >= PACK * i, 1, 0) for i in range(1, 4)])
+    inner = sum([jnp.where(here - outer * PACK >= CAP * i, 1, 0) for i in range(1, 4)])
+    there = lax.broadcasted_iota(jnp.int32, (4 * PACK, 4 * PACK), 1)
+    turn[...] = jnp.where(there == here + (inner - outer) * (PACK - CAP), 1.0, 0.0).astype(BF16)
 
     def compacted(i):
-        xb[0, 0, 0, i] = dot(compact, d1[i].reshape(8 * SLOT, HALF)).astype(BF16)
+        for g in range(2):
+            turned = dot(turn[...], d1[i, 4 * g : 4 * g + 4].reshape(4 * PACK, 128)).astype(BF16)
+            for j in range(4):
+                xb[0, 0, 0, i, PACK * g : PACK * g + PACK, 128 * j : 128 * j + 128] = turned[
+                    PACK * j : PACK * j + PACK
+                ]
 
     got = {}
 
@@ -286,6 +293,18 @@
         accg[side, dy] += dot_t(a, wg[:, low]) + dot_t(b, wg[:, high])
         accu[side, dy] += dot_t(a, wu[:, low]) + dot_t(b, wu[:, high])
 
+    hid_n = {}
+
+    def hide(side, dy):
+        g = accg[side, dy]
+        hid[0, side, dy] = (g / (1.0 + jnp.exp(-g)) * accu[side, dy]).astype(BF16)
+        n = hid_n[1 - side, dy] = sems.take()
+        push(hid.at[0, side, dy], hid.at[1, 1 - side, dy], n, mate)
+
+    def shared(dy):
+        for side in range(2):
+            arrive(hid.at[1, side, dy], hid_n[side, dy])
+
     own = [(0, 0, 0, 0), (0, 0, 0, 1)]
     pl.loop(1, 8)(lambda r: dispatched(0, r))
     compacted(0)
@@ -297,6 +316,14 @@
     pl.loop(0, 8)(lambda r: dispatched(1, r))
     compacted(1)
     relay(own[1], "l"), relay(own[1], "r"), relay(own[1], "y"), relay(own[1], "m")
+    lanes = lax.broadcasted_iota(jnp.int32, (128, EXPERTS * PACK), 1).astype(F32)
+    first = gates / 65536.0
+    for j in range(4):
+        weights = jnp.where(lanes == slot0 + CAP * j, first, 0.0)
+        weights += jnp.where(lanes == slot1 + CAP * j, 1.0 - first, 0.0)
+        coarse = weights.astype(BF16)
+        cw[0, 128 * j : 128 * j + 128] = coarse
+        cw[1, 128 * j : 128 * j + 128] = (weights - coarse.astype(F32)).astype(BF16)
     landed((0, 0, 3, 0)), relay((0, 0, 3, 0), "r")
     landed((0, 1, 0, 0)), relay((0, 1, 0, 0), "r"), relay((0, 1, 0, 0), "l")
     multiply(0, 0, 0)
@@ -325,23 +352,17 @@
     multiply(0, 1, 3)
     landed((1, 0, 2, 0)), landed((1, 0, 2, 1))
     multiply(1, 0, 2)
+    hide(0, 0), hide(1, 0)
     landed((0, 1, 2, 0), 0), landed((0, 1, 2, 0), 1), relay((0, 1, 2, 0), "m")
     landed((0, 1, 2, 1)), relay((0, 1, 2, 1), "m")
-    multiply(0, 1, 2)
-    for slot in ((1, 1), (1, 3), (1, 2)):
+    for slot in ((1, 1), (1, 3)):
         landed((1, *slot, 0)), landed((1, *slot, 1))
         multiply(1, *slot)
-
-    hid_n = {}
-    for side, dy in ((0, 0), (1, 0), (0, 1), (1, 1)):
-        g = accg[side, dy]
-        hid[0, side, dy] = (g / (1.0 + jnp.exp(-g)) * accu[side, dy]).astype(BF16)
-        n = hid_n[1 - side, dy] = sems.take()
-        push(hid.at[0, side, dy], hid.at[1, 1 - side, dy], n, mate)
-    loads[2].wait()
-    wd_move.wait()
-    for (side, dy), n in hid_n.items():
-        arrive(hid.at[1, side, dy], n)
+    multiply(0, 1, 2)
+    landed((1, 1, 2, 0)), landed((1, 1, 2, 1))
+    multiply(1, 1, 2)
+
+    hide(0, 1), hide(1, 1)
 
     def down(dy, dx):
         columns = pl.ds(pl.multiple_of(lax.rem(x + dx, 4) * HALF, HALF), HALF)
@@ -365,12 +386,16 @@
         for ref, n in terms:
             arrive(ref, n)
 
+    loads[2].wait()
+    wd_move.wait()
+    shared(0)
+    down(0, 2)
+    from_r_2 = give(yb.at[0, 2, 0], rh.at[1], left)
+    shared(1)
     down(1, 2)
     from_y2 = give(yb.at[1, 2, 1], rh.at[0], across)
     from_r_q = give(yb.at[1, 2, 0, pl.ds(0, QUARTER)], rq.at[0], left)
     from_l_q = give(yb.at[1, 2, 0, pl.ds(QUARTER, QUARTER)], rq.at[1], right)
-    down(0, 2)
-    from_r_2 = give(yb.at[0, 2, 0], rh.at[1], left)
     down(1, 3)
     from_y_3 = give(yb.at[1, 3, 1], rh.at[2], across)
     down(1, 1)
@@ -401,12 +426,10 @@
     last_y[0] = give(yb.at[1, 0, 0], rf.at[1, 0], across)
     down(0, 0)
 
-    wide = lax.broadcasted_iota(jnp.int32, (8 * SLOT, ROWS), 0)
-    tight = lax.broadcasted_iota(jnp.int32, (8 * SLOT, ROWS), 1)
-    block = sum([jnp.where(tight >= CAP * i, 1, 0) for i in range(1, 8)])
-    spread = jnp.where(wide == tight + block * (SLOT - CAP), 1.0, 0.0).astype(BF16)
     r2_n = sems.take(16)
     r2_s = sems.take(16)
+
+    far = lax.rem(zh + core, 2)
 
     def back(i, r):
         s = lax.rem(me8 + r, 8)
@@ -414,8 +437,8 @@
             zl_=lax.div(s, 2), yh_=lax.rem(s, 2), core_=core if i == 0 else 1 - core, zh_=core
         )
         return pltpu.make_async_remote_copy(
-            src_ref=r2s.at[i, s], dst_ref=r2.at[zh, me8],
-            send_sem=send.at[r2_s + 8 * i + r], recv_sem=recv.at[r2_n + zh * 8 + me8],
+            src_ref=r2s.at[i, s], dst_ref=r2.at[far, me8],
+            send_sem=send.at[r2_s + 8 * i + r], recv_sem=recv.at[r2_n + far * 8 + me8],
             device_id=device, device_id_type=MESH,
         )
 
@@ -427,12 +450,14 @@
             + rf[1, i].astype(F32)
             + rf[2, i].astype(F32)
         ).astype(BF16)
-        r2s[i] = dot(spread, value).astype(BF16).reshape(8, SLOT, HALF)
+        for g in range(2):
+            turned = dot(turn[...], fold(value[PACK * g : PACK * g + PACK]))
+            r2s[i, 4 * g : 4 * g + 4] = turned.astype(BF16).reshape(4, PACK, 128)
         if i == 0:
 
             @pl.when(core == zh)
             def _():
-                r2[zh, me8] = r2s[0, me8]
+                r2[0, me8] = r2s[0, me8]
 
             @pl.when(core != zh)
             def _():
@@ -442,19 +467,24 @@
         else:
             pl.loop(0, 8)(lambda r: back(1, r).start())
 
-    @pl.loop(1, 16)
-    def _(r):
-        j = lax.rem(mine + r, 16)
-        arrive(r2.at[lax.div(j, 8), lax.rem(j, 8)], r2_n + j)
+    def weighted(i):
+        back_rows = r2[i].reshape(EXPERTS * PACK, 128)
+        mixed = dot(cw[0], back_rows) + dot(cw[1], back_rows)
+        return jnp.concatenate([mixed[128 * j : 128 * j + 128] for j in range(4)], axis=1)
+
+    def returned(i, r):
+        e = lax.rem(me8 + r, 8)
+        arrive(r2.at[i, e], r2_n + 8 * i + e)
+
+    pl.loop(1, 8)(lambda r: returned(0, r))
 
     @pl.when(core != zh)
     def _():
-        arrive(r2.at[zh, me8], r2_n + mine)
-
-    mix = stream[...]
-    for i in range(2):
-        back_rows = r2[i].reshape(8 * SLOT, HALF)
-        mix += dot(cw[0], back_rows) + dot(cw[1], back_rows)
+        returned(0, 0)
+
+    mix = stream[...] + weighted(0)
+    pl.loop(0, 8)(lambda r: returned(1, r))
+    mix += weighted(1)
     out_ref[...] = mix.astype(BF16)
 
     for src, n in started:
@@ -504,10 +534,11 @@
             pltpu.VMEM((2, 4, 4, 272, 128), BF16),
             pltpu.VMEM((8, 8, 128), F32),
             pltpu.VMEM((128, HALF), F32),
-            pltpu.VMEM((128, EXPERTS * SLOT), BF16),
-            pltpu.VMEM((2, 128, EXPERTS * SLOT), BF16),
-            pltpu.VMEM((EXPERTS, SLOT, HALF), BF16),
-            pltpu.VMEM((2, 8, SLOT, HALF), BF16),
+            pltpu.VMEM((EXPERTS * PACK, HALF), BF16),
+            pltpu.VMEM((2, HALF, EXPERTS * PACK), BF16),
+            pltpu.VMEM((4 * PACK, 4 * PACK), BF16),
+            pltpu.VMEM((EXPERTS, PACK, 128), BF16),
+            pltpu.VMEM((2, 8, PACK, 128), BF16),
             pltpu.VMEM((2, 2, 4, 2, ROWS, HALF), BF16),
             pltpu.VMEM(w_gate.shape[::-1], BF16),
             pltpu.VMEM(w_up.shape[::-1], BF16),
@@ -519,8 +550,8 @@
             pltpu.VMEM((2, QUARTER, HALF), BF16),
             pltpu.VMEM((7, ROWS, HALF), BF16),
             pltpu.VMEM((3, 2, ROWS, HALF), BF16),
-            pltpu.VMEM((2, 8, SLOT, HALF), BF16),
-            pltpu.VMEM((2, 8, SLOT, HALF), BF16),
+            pltpu.VMEM((2, 8, PACK, 128), BF16),
+            pltpu.VMEM((2, 8, PACK, 128), BF16),
             pltpu.SemaphoreType.DMA((SEMS,)),
             pltpu.SemaphoreType.DMA((SEMS,)),
             pltpu.SemaphoreType.DMA((3,)),

time: 154 us -> 146 us (0.948)
  Pallas kernels: 151 us -> 143 us
    pallas_call x1, Pallas kernels: 151 us -> 143 us  [body(): pl.pallas_call(kernel, out_shape=jax.ShapeDtypeStruct(residual.shape, BF1...]
where the time goes in v3:
time: 146 us
  Pallas kernels  143 us (98%)
  local copies, waits for them, and re-layouts  2.83 us (2%)
    pallas_call x1, Pallas kernels, body(): pl.pallas_call(kernel, out_shape=jax.ShapeDtypeStruct(residual.shape, BF1...  143 us

profile of v3, /device:TPU:33, one launch (start us, length us, event | category | flops | bytes accessed | tf_op | source)
XLA Modules:
  0.0 146.0 jit_solution(2175709949380577817)
XLA Ops:
  0.0 1.3 reshape.11.gain_ref
  1.3 143.2 %shard_map.109 = bf16[128,512]{1,0:T(8,128)(2,1)} custom-call(bf16[128,512]{1,0:T(8,128)(2,1)} %q_ref.1, bf16[128,128]{1,0:T(8,128)(2,1)} %k_ref.1, bf16[128,128]{1,0:T(8,128)(2,1)} %v_ref.1, s32[2,128]{1,0:T(2,128)} %bitcast.7, s32[1,128]{1,0:T(1,128)} %bitcast.8, s32[1,128]{1,0:T(1,128)} %bitcast.9, bf16[128,512]{1,0:T(8,128)(2,1)} %resid_ref.1, ...), custom_call_target="tpu_custom_call" | custom-call | flops 14000000000 | bytes 12000000 | tf_op jit(solution)/shard_map/pallas_call | solution.py:528
  144.5 1.6 %copy.13 = bf16[128,512]{1,0:T(8,128)(2,1)} copy(bf16[128,512]{1,0:T(8,128)(2,1)} %shard_map.109) | data formatting | bytes 262144

commit v4 on v3

--- a/solution.py
+++ b/solution.py
@@ -230,7 +230,9 @@
 
     all_sq = jnp.sum(ssq[...], axis=0)
     all_sq = jnp.transpose(jnp.concatenate([all_sq] * 16, axis=0))[:, 0:1]
-    normed = flow * lax.rsqrt(all_sq / 4096.0 + 1e-05) * gain_ref[...].astype(F32)
+    gains = gain_ref[...].astype(F32)
+    gains = jnp.concatenate([gains[j : j + 1] for j in range(4)], axis=1)
+    normed = flow * lax.rsqrt(all_sq / 4096.0 + 1e-05) * gains
     rows = dot(pick[...], fold(normed.astype(BF16)))
     gbuf[...] = rows.astype(BF16).reshape(EXPERTS, PACK, 128)
 
@@ -564,7 +566,7 @@
         ),
     )(
         query_rows, key_head_rows, value_head_rows, expert_ids.T, gate_fixed.reshape(1, -1),
-        positions.reshape(1, -1), residual, norm_gain.reshape(1, -1), w_gate.T, w_up.T, w_down,
+        positions.reshape(1, -1), residual, norm_gain.reshape(4, -1), w_gate.T, w_up.T, w_down,
     )
 
 

time: 146 us -> 145 us (level)
  no operation moved by 1% of the time
where the time goes in v4:
time: 145 us
  Pallas kernels  143 us (99%)
  local copies, waits for them, and re-layouts  1.57 us (1%)
    pallas_call x1, Pallas kernels, body(): pl.pallas_call(kernel, out_shape=jax.ShapeDtypeStruct(residual.shape, BF1...  143 us

profile of v4, /device:TPU:33, one launch (start us, length us, event | category | flops | bytes accessed | tf_op | source)
XLA Modules:
  0.0 144.8 jit_solution(13537093655307269239)
XLA Ops:
  0.0 143.3 %shard_map.109 = bf16[128,512]{1,0:T(8,128)(2,1)} custom-call(bf16[128,512]{1,0:T(8,128)(2,1)} %q_ref.1, bf16[128,128]{1,0:T(8,128)(2,1)} %k_ref.1, bf16[128,128]{1,0:T(8,128)(2,1)} %v_ref.1, s32[2,128]{1,0:T(2,128)} %bitcast.8, s32[1,128]{1,0:T(1,128)} %bitcast.10, s32[1,128]{1,0:T(1,128)} %bitcast.11, bf16[128,512]{1,0:T(8,128)(2,1)} %resid_ref.1, ...), custom_call_target="tpu_custom_call" | custom-call | flops 14000000000 | bytes 12000000 | tf_op jit(solution)/shard_map/pallas_call | solution.py:530
  143.3 1.6 %copy.13 = bf16[128,512]{1,0:T(8,128)(2,1)} copy(bf16[128,512]{1,0:T(8,128)(2,1)} %shard_map.109) | data formatting | bytes 262144
